TPU v7x, 512 devices: a whole 4x4x16 slice. The times are simulated.
512 devices in a mesh: coil: 16 (over z_lo, core), slab: 32 (over x, z_hi, y).
Axes of the slice: x: 4, y: 4, z: 16 (z_hi: 2, z_lo: 8; z = z_hi * 8 + z_lo), core: 2. Of those that a mesh axis runs over, the one named last changes fastest.
Arguments:
- kspace_data: bfloat16 [32, 2, 128, 128, 128], P('coil', None, None, 'slab'), may hold values from -4 to 4
- coil_maps: bfloat16 [32, 2, 128, 128, 128], P('coil', None, 'slab'), may hold values from -1.796875 to 1.796875
- sample_mask: int32 [32, 128, 128], P('coil', None, 'slab'), may hold values 0 or 1
- initial_image: float32 [2, 128, 128, 128], P(None, 'slab', 'coil'), may hold values from -6 to 6
Outputs:
- image: float32 [2, 128, 128, 128], P(None, 'slab', 'coil')
All inputs are finite; a program needn't handle non-finite values. No bound on the sum of `sample_mask` on one device may be relied on, other than what follows from the above.
Results may differ from a plain program's by a relative error of at most 0.0045.
Values may be sent and summed in bfloat16 or wider, within the bound.
No kernel may reach another device: no remote copies, remote signals or barrier semaphores. Data moves between devices by JAX's collectives and lax.ppermute only.
A program may use at most 64 MiB of HBM per device.

v0:
```python
import math
import jax
import jax.numpy as jnp
from jax import lax
from jax.sharding import PartitionSpec as P

NX = 128
NY = 128
NZ = 128
ITERS = 2
dual_step = 0.25
primal_step = 0.25
tv_weight = 0.5


def from_behind(block, axis, distance):
    devices = range(lax.axis_size(axis))
    route = [(i - distance, i) for i in devices if i - distance in devices]
    return lax.ppermute(block, axis, route)


def in_blocks(shard, dim, size):
    before, after = (shard.shape[:dim], shard.shape[dim + 1 :])
    return jnp.moveaxis(shard.reshape(*before, size, -1, *after), dim, 0)


def sum_at_owner(shard, axis, dim):
    tiles = in_blocks(shard, dim, lax.axis_size(axis))
    arrived = lax.all_to_all(tiles, axis, split_axis=0, concat_axis=0, tiled=True)
    return arrived.sum(axis=0)


def dft_table(length, inverse):
    counter = jnp.arange(length, dtype=jnp.int32)
    product = counter[:, None] * counter[None, :] % length
    phase = 2.0 * math.pi / length * product.astype(jnp.float32)
    scale = 1.0 / math.sqrt(length)
    real_part = jnp.cos(phase) * scale
    imag_part = jnp.sin(phase) * scale
    if not inverse:
        imag_part = -imag_part
    table = jnp.stack([jnp.stack([real_part, imag_part]), jnp.stack([-imag_part, real_part])])
    return table.astype(jnp.bfloat16)


def data_term(guess, coil_maps, kspace_data, sample_mask, dual_data, tables):
    forward_x, forward_y, forward_z, inverse_x, inverse_y, inverse_z = tables
    maps_real = coil_maps[:, 0].astype(jnp.float32)
    maps_imag = coil_maps[:, 1].astype(jnp.float32)
    pieces = jnp.stack(
        [maps_real * guess[0] - maps_imag * guess[1], maps_real * guess[1] + maps_imag * guess[0]],
        1,
    ).astype(jnp.bfloat16)
    pieces = jnp.einsum(
        "ckzyx,kjxw->cjzyw", pieces, forward_x, preferred_element_type=jnp.float32
    ).astype(jnp.bfloat16)
    pieces = jnp.einsum(
        "ckzyx,kjyv->cjzvx", pieces, forward_y, preferred_element_type=jnp.float32
    ).astype(jnp.bfloat16)
    spectrum = jnp.einsum(
        "ckzyx,kjzw->cjwyx",
        lax.all_to_all(pieces, "slab", split_axis=3, concat_axis=2, tiled=True),
        forward_z,
        preferred_element_type=jnp.float32,
    )
    sampled = sample_mask[:, None, :, :, None].astype(jnp.float32)
    dual_new = (
        dual_data + dual_step * (sampled * (spectrum - kspace_data.astype(jnp.float32)))
    ) / (1.0 + dual_step)
    back_field = jnp.einsum(
        "ckzyx,kjzw->cjwyx",
        dual_new.astype(jnp.bfloat16),
        inverse_z,
        preferred_element_type=jnp.float32,
    ).astype(jnp.bfloat16)
    back_field = jnp.einsum(
        "ckzyx,kjyv->cjzvx",
        lax.all_to_all(back_field, "slab", split_axis=2, concat_axis=3, tiled=True),
        inverse_y,
        preferred_element_type=jnp.float32,
    ).astype(jnp.bfloat16)
    back_field = jnp.einsum(
        "ckzyx,kjxw->cjzyw", back_field, inverse_x, preferred_element_type=jnp.float32
    )
    real_sum = jnp.sum(maps_real * back_field[:, 0] + maps_imag * back_field[:, 1], 0)
    imag_sum = jnp.sum(maps_real * back_field[:, 1] - maps_imag * back_field[:, 0], 0)
    return (jnp.stack([real_sum, imag_sum]), dual_new)


def tv_update(guess, duals):
    planes = guess.shape[1]
    plane_pos = lax.axis_index("slab") * planes + lax.broadcasted_iota(
        jnp.int32, (1, planes, 1, 1), 1
    )
    next_plane = from_behind(guess[:, :1], "slab", -1)
    ahead_z = jnp.concatenate([guess[:, 1:], next_plane], 1)
    grad_z = jnp.where(plane_pos < NZ - 1, ahead_z - guess, 0.0)
    grad_y = jnp.concatenate(
        [guess[:, :, 1:] - guess[:, :, :-1], jnp.zeros_like(guess[:, :, :1])], 2
    )
    grad_x = jnp.concatenate([guess[..., 1:] - guess[..., :-1], jnp.zeros_like(guess[..., :1])], 3)
    moved_z = duals[0] + dual_step * grad_z
    moved_y = duals[1] + dual_step * grad_y
    moved_x = duals[2] + dual_step * grad_x
    magnitude = jnp.sqrt(
        jnp.sum(moved_z * moved_z, 0)
        + jnp.sum(moved_y * moved_y, 0)
        + jnp.sum(moved_x * moved_x, 0)
    )
    factor = 1.0 / jnp.maximum(1.0, magnitude / tv_weight)
    dual_z = moved_z * factor
    dual_y = moved_y * factor
    dual_x = moved_x * factor
    prior_plane = from_behind(dual_z[:, -1:], "slab", 1)
    spread_z = jnp.concatenate([prior_plane, dual_z[:, :-1]], 1) - dual_z
    spread_y = jnp.concatenate([jnp.zeros_like(dual_y[:, :, :1]), dual_y[:, :, :-1]], 2) - dual_y
    spread_x = jnp.concatenate([jnp.zeros_like(dual_x[..., :1]), dual_x[..., :-1]], 3) - dual_x
    return ((dual_z, dual_y, dual_x), spread_z + spread_y + spread_x)


def on_device(kspace_data, coil_maps, sample_mask, initial_image):
    tables = (
        dft_table(NX, False),
        dft_table(NY, False),
        dft_table(NZ, False),
        dft_table(NX, True),
        dft_table(NY, True),
        dft_table(NZ, True),
    )
    dual_data = jnp.zeros(kspace_data.shape, jnp.float32)
    share_rows = initial_image.shape[2]
    current = initial_image
    guess = current
    duals = None
    for turn_index in range(ITERS):
        whole_guess = lax.all_gather(guess, "coil", axis=2, tiled=True)
        if duals is None:
            duals = (
                jnp.zeros_like(whole_guess),
                jnp.zeros_like(whole_guess),
                jnp.zeros_like(whole_guess),
            )
        data_grad, dual_data = data_term(
            whole_guess, coil_maps, kspace_data, sample_mask, dual_data, tables
        )
        data_grad = sum_at_owner(data_grad, "coil", 2)
        duals, spread = tv_update(whole_guess, duals)
        spread_share = lax.dynamic_slice_in_dim(
            spread, lax.axis_index("coil") * share_rows, share_rows, 2
        )
        updated = current - primal_step * (data_grad + spread_share)
        guess = 2.0 * updated - current
        current = updated
    return current


def solution(mesh):
    placed = (
        P("coil", None, None, "slab", None),
        P("coil", None, "slab", None, None),
        P("coil", None, "slab"),
        P(None, "slab", "coil", None),
    )
    return jax.shard_map(
        on_device,
        mesh=mesh,
        in_specs=placed,
        out_specs=P(None, "slab", "coil", None),
        check_vma=False,
    )
```

profile of v0, /device:TPU:130, one launch (start us, length us, event | category | flops | bytes accessed | tf_op | source)
XLA Modules:
  0.0 341.5 jit_solution(4469572003324194506)
XLA Ops:
  0.0 0.3 negate_convert_fusion
  0.3 0.0 copy-start.6
  0.3 0.3 fusion.85
  0.6 0.5 copy-done.6
  1.0 20.8 %all_gather.6 = f32[2,4,128,128]{3,2,1,0:T(8,128)S(1)} all-gather(f32[2,4,8,128]{3,2,1,0:T(8,128)S(1)} %copy-done.6), channel_id=1, replica_groups=mesh['coil'=16,'slab'=32] {'coil'}, dimensions={2}, use_global_device_ids=true | all-gather | bytes 557056 | tf_op jit(solution)/shard_map/all_gather | solution.py:136
  21.8 1.0 copy-done.2
  22.8 0.2 fusion.24
  23.1 0.6 fusion.21
  23.6 1.2 copy.77
  24.8 13.6 %all-to-all-start = ((bf16[2,2,4,128,128]{4,2,0,1,3:T(4,128)(2,1)}), bf16[2,2,4,128,128]{4,2,0,1,3:T(4,128)(2,1)S(1)}, u32[]{:S(2)}, u32[]{:S(2)}) async-start(bf16[2,2,4,128,128]{4,2,0,1,3:T(4,128)(2,1)} %copy.77), calls=%async_computation | async-start | bytes 1048576 | tf_op jit(solution)/shard_map/all_to_all | solution.py:62
  38.5 19.4 %all-to-all-done = bf16[2,2,4,128,128]{4,2,0,1,3:T(4,128)(2,1)S(1)} async-done(((bf16[2,2,4,128,128]{4,2,0,1,3:T(4,128)(2,1)}), bf16[2,2,4,128,128]{4,2,0,1,3:T(4,128)(2,1)S(1)}, u32[]{:S(2)}, u32[]{:S(2)}) %all-to-all-start) | async-done | bytes 524320 | tf_op jit(solution)/shard_map/all_to_all | solution.py:62
  57.9 0.2 copy.78
  58.2 0.8 copy-done.4
  58.9 1.3 fusion.105
  60.3 0.3 fusion.20
  60.6 0.4 copy.82
  61.0 33.9 %all_to_all.82 = bf16[2,2,128,4,128]{4,3,0,1,2:T(4,128)(2,1)S(1)} all-to-all(bf16[2,2,128,4,128]{4,3,0,1,2:T(4,128)(2,1)S(1)} %copy.82), channel_id=1, replica_groups=mesh['coil'=16,'slab'=32] {'slab'}, dimensions={2} | all-to-all | bytes 1048576 | tf_op jit(solution)/shard_map/all_to_all | solution.py:78
  94.9 0.2 copy.83
  95.2 0.5 convolution_bitcast_fusion.2
  95.7 0.2 fusion.28
  95.9 0.9 copy.92
  96.8 26.0 %all-to-all-start.2 = ((f32[16,2,4,8,128]{4,3,2,1,0:T(8,128)}), f32[16,2,4,8,128]{4,3,2,1,0:T(8,128)}, u32[]{:S(2)}, u32[]{:S(2)}) async-start(f32[16,2,4,8,128]{4,3,2,1,0:T(8,128)} %copy.92), calls=%async_computation.2 | async-start | bytes 1048576 | tf_op jit(solution)/shard_map/all_to_all | solution.py:29
  122.8 9.0 %collective-permute-start = (f32[2,1,128,128]{3,2,1,0:T(8,128)S(1)}, f32[2,1,128,128]{3,2,1,0:T(8,128)S(1)}, u32[]{:S(2)}, u32[]{:S(2)}) collective-permute-start(f32[2,1,128,128]{3,2,1,0:T(8,128)S(1)} %slice.135), channel_id=1, source_target_pairs={{1,0},{2,1},{3,2},{4,3},{5,4},{6,5},{7,6},{8,7},{9,8},{10,9},{11,1... | collective-permute-start | bytes 393224 | tf_op jit(solution)/shard_map/ppermute | solution.py:19
  131.9 0.2 slice_subtract_fusion.2
  132.1 0.1 slice_subtract_fusion.3
  132.2 0.1 multiply_reduce_fusion.3
  132.3 23.6 %collective-permute-done = f32[2,1,128,128]{3,2,1,0:T(8,128)S(1)} collective-permute-done((f32[2,1,128,128]{3,2,1,0:T(8,128)S(1)}, f32[2,1,128,128]{3,2,1,0:T(8,128)S(1)}, u32[]{:S(2)}, u32[]{:S(2)}) %collective-permute-start) | collective-permute-done | bytes 131104 | tf_op jit(solution)/shard_map/ppermute | solution.py:19
  155.9 0.2 multiply_reduce_fusion.5
  156.1 0.1 divide_multiply_fusion
  156.2 0.3 broadcast_multiply_fusion.3
  156.5 1.9 collective-permute-start.1
  158.5 0.0 all-to-all-done.2
  158.5 1.1 reduce_sum.110
  159.6 18.0 %collective-permute-done.1 = f32[2,1,128,128]{3,2,1,0:T(8,128)S(1)} collective-permute-done((f32[2,1,128,128]{3,2,1,0:T(8,128)S(1)}, f32[2,1,128,128]{3,2,1,0:T(8,128)S(1)}, u32[]{:S(2)}, u32[]{:S(2)}) %collective-permute-start.1) | collective-permute-done | bytes 131104 | tf_op jit(solution)/shard_map/ppermute | solution.py:19
  177.6 0.1 multiply_subtract_fusion.1
  177.6 15.8 %all_gather.7 = f32[2,4,128,128]{3,2,1,0:T(8,128)S(1)} all-gather(f32[2,4,8,128]{3,2,1,0:T(8,128)S(1)} %get-tuple-element.11), channel_id=1, replica_groups=mesh['coil'=16,'slab'=32] {'coil'}, dimensions={2}, use_global_device_ids=true | all-gather | bytes 557056 | tf_op jit(solution)/shard_map/all_gather | solution.py:136
  193.4 1.0 fusion.32
  194.4 2.4 fusion.18
  196.8 1.4 copy.94
  198.3 35.9 %all_to_all.83 = bf16[2,2,4,128,128]{4,2,0,1,3:T(4,128)(2,1)S(1)} all-to-all(bf16[2,2,4,128,128]{4,2,0,1,3:T(4,128)(2,1)S(1)} %copy.94), channel_id=1, replica_groups=mesh['coil'=16,'slab'=32] {'slab'}, dimensions={3} | all-to-all | bytes 1048576 | tf_op jit(solution)/shard_map/all_to_all | solution.py:62
  234.3 0.2 copy.95
  234.5 0.8 copy-done.5
  235.3 0.4 fusion.6
  235.7 0.3 fusion.17
  236.0 0.4 copy.99
  236.4 26.2 %all_to_all.84 = bf16[2,2,128,4,128]{4,3,0,1,2:T(4,128)(2,1)S(1)} all-to-all(bf16[2,2,128,4,128]{4,3,0,1,2:T(4,128)(2,1)S(1)} %copy.99), channel_id=1, replica_groups=mesh['coil'=16,'slab'=32] {'slab'}, dimensions={2} | all-to-all | bytes 1048576 | tf_op jit(solution)/shard_map/all_to_all | solution.py:78
  262.7 1.1 copy.100
  263.8 2.5 convolution_bitcast_fusion
  266.3 1.4 fusion.36
  267.8 0.9 copy.109
  268.7 18.8 %all-to-all-start.5 = ((f32[16,2,4,8,128]{4,3,2,1,0:T(8,128)}), f32[16,2,4,8,128]{4,3,2,1,0:T(8,128)}, u32[]{:S(2)}, u32[]{:S(2)}) async-start(f32[16,2,4,8,128]{4,3,2,1,0:T(8,128)} %copy.109), calls=%async_computation.5 | async-start | bytes 1048576 | tf_op jit(solution)/shard_map/all_to_all | solution.py:29
  287.5 10.7 %collective-permute-start.2 = (f32[2,1,128,128]{3,2,1,0:T(8,128)S(1)}, f32[2,1,128,128]{3,2,1,0:T(8,128)S(1)}, u32[]{:S(2)}, u32[]{:S(2)}) collective-permute-start(f32[2,1,128,128]{3,2,1,0:T(8,128)S(1)} %slice.149), channel_id=1, source_target_pairs={{1,0},{2,1},{3,2},{4,3},{5,4},{6,5},{7,6},{8,7},{9,8},{10,9},{11,1... | collective-permute-start | bytes 393224 | tf_op jit(solution)/shard_map/ppermute | solution.py:19
  298.1 0.2 slice_subtract_fusion
  298.3 0.1 multiply_reduce_fusion
  298.4 0.1 slice_subtract_fusion.1
  298.5 0.1 multiply_reduce_fusion.1
  298.6 21.9 %collective-permute-done.2 = f32[2,1,128,128]{3,2,1,0:T(8,128)S(1)} collective-permute-done((f32[2,1,128,128]{3,2,1,0:T(8,128)S(1)}, f32[2,1,128,128]{3,2,1,0:T(8,128)S(1)}, u32[]{:S(2)}, u32[]{:S(2)}) %collective-permute-start.2) | collective-permute-done | bytes 131104 | tf_op jit(solution)/shard_map/ppermute | solution.py:19
  320.5 0.2 multiply_reduce_fusion.2
  320.7 0.1 maximum_divide_fusion
  320.8 0.3 broadcast_multiply_fusion.2
  321.1 1.9 collective-permute-start.3
  323.1 1.1 reduce_sum.116
  324.2 16.7 %collective-permute-done.3 = f32[2,1,128,128]{3,2,1,0:T(8,128)S(1)} collective-permute-done((f32[2,1,128,128]{3,2,1,0:T(8,128)S(1)}, f32[2,1,128,128]{3,2,1,0:T(8,128)S(1)}, u32[]{:S(2)}, u32[]{:S(2)}) %collective-permute-start.3) | collective-permute-done | bytes 131104 | tf_op jit(solution)/shard_map/ppermute | solution.py:19
  340.8 0.7 multiply_subtract_fusion
  (28 shorter events, 0.3 us)
Async XLA Ops:
  0.3 0.8 copy-start.6
  21.8 1.0 copy-start.2
  24.8 13.6 %copy-start.7 = (s32[2,128,4]{1,2,0:T(4,128)S(1)}, s32[2,128,4]{1,2,0:T(4,128)}, u32[]{:S(2)}) copy-start(s32[2,128,4]{1,2,0:T(4,128)} %param.6) | copy-start | bytes 12292
  24.8 33.1 %all-to-all-start = ((bf16[2,2,4,128,128]{4,2,0,1,3:T(4,128)(2,1)}), bf16[2,2,4,128,128]{4,2,0,1,3:T(4,128)(2,1)S(1)}, u32[]{:S(2)}, u32[]{:S(2)}) async-start(bf16[2,2,4,128,128]{4,2,0,1,3:T(4,128)(2,1)} %copy.77), calls=%async_computation | async-start | bytes 1048576 | tf_op jit(solution)/shard_map/all_to_all | solution.py:62
  57.9 1.0 copy-start.4
  96.8 61.7 %all-to-all-start.2 = ((f32[16,2,4,8,128]{4,3,2,1,0:T(8,128)}), f32[16,2,4,8,128]{4,3,2,1,0:T(8,128)}, u32[]{:S(2)}, u32[]{:S(2)}) async-start(f32[16,2,4,8,128]{4,3,2,1,0:T(8,128)} %copy.92), calls=%async_computation.2 | async-start | bytes 1048576 | tf_op jit(solution)/shard_map/all_to_all | solution.py:29
  122.8 33.0 %collective-permute-start = (f32[2,1,128,128]{3,2,1,0:T(8,128)S(1)}, f32[2,1,128,128]{3,2,1,0:T(8,128)S(1)}, u32[]{:S(2)}, u32[]{:S(2)}) collective-permute-start(f32[2,1,128,128]{3,2,1,0:T(8,128)S(1)} %slice.135), channel_id=1, source_target_pairs={{1,0},{2,1},{3,2},{4,3},{5,4},{6,5},{7,6},{8,7},{9,8},{10,9},{11,1... | collective-permute-start | bytes 393224 | tf_op jit(solution)/shard_map/ppermute | solution.py:19
  156.5 21.0 %collective-permute-start.1 = (f32[2,1,128,128]{3,2,1,0:T(8,128)S(1)}, f32[2,1,128,128]{3,2,1,0:T(8,128)S(1)}, u32[]{:S(2)}, u32[]{:S(2)}) collective-permute-start(f32[2,1,128,128]{3,2,1,0:T(8,128)S(1)} %slice.140), channel_id=1, source_target_pairs={{0,1},{1,2},{2,3},{3,4},{4,5},{5,6},{6,7},{7,8},{8,9},{9,10},{10,1... | collective-permute-start | bytes 393224 | tf_op jit(solution)/shard_map/ppermute | solution.py:19
  193.4 105.0 %copy-start = (f32[2,4,128,128]{3,2,1,0:T(8,128)}, f32[2,4,128,128]{3,2,1,0:T(8,128)S(1)}, u32[]{:S(2)}) copy-start(f32[2,4,128,128]{3,2,1,0:T(8,128)S(1)} %all_gather.7) | copy-start | bytes 1572868
  198.3 36.2 %copy-start.3 = (f32[2,2,128,4,128]{4,2,3,0,1:T(8,128)S(1)}, f32[2,2,128,4,128]{4,2,3,0,1:T(8,128)}, u32[]{:S(2)}) copy-start(f32[2,2,128,4,128]{4,2,3,0,1:T(8,128)} %get-tuple-element.34) | copy-start | bytes 3145732
  234.3 1.0 copy-start.5
  268.7 54.4 %all-to-all-start.5 = ((f32[16,2,4,8,128]{4,3,2,1,0:T(8,128)}), f32[16,2,4,8,128]{4,3,2,1,0:T(8,128)}, u32[]{:S(2)}, u32[]{:S(2)}) async-start(f32[16,2,4,8,128]{4,3,2,1,0:T(8,128)} %copy.109), calls=%async_computation.5 | async-start | bytes 1048576 | tf_op jit(solution)/shard_map/all_to_all | solution.py:29
  287.5 33.0 %collective-permute-start.2 = (f32[2,1,128,128]{3,2,1,0:T(8,128)S(1)}, f32[2,1,128,128]{3,2,1,0:T(8,128)S(1)}, u32[]{:S(2)}, u32[]{:S(2)}) collective-permute-start(f32[2,1,128,128]{3,2,1,0:T(8,128)S(1)} %slice.149), channel_id=1, source_target_pairs={{1,0},{2,1},{3,2},{4,3},{5,4},{6,5},{7,6},{8,7},{9,8},{10,9},{11,1... | collective-permute-start | bytes 393224 | tf_op jit(solution)/shard_map/ppermute | solution.py:19
  298.5 22.0 %copy-start.1 = (f32[2,4,128,128]{3,2,1,0:T(8,128)S(1)}, f32[2,4,128,128]{3,2,1,0:T(8,128)}, u32[]{:S(2)}) copy-start(f32[2,4,128,128]{3,2,1,0:T(8,128)} %copy-done) | copy-start | bytes 1572868
  298.5 22.0 %slice-start = ((f32[2,4,128,128]{3,2,1,0:T(8,128)}), f32[2,3,128,128]{3,2,1,0:T(8,128)S(1)}, s32[]{:S(2)}) async-start(f32[2,4,128,128]{3,2,1,0:T(8,128)} %copy-done), calls=%async_computation.6 | async-start | bytes 786432 | tf_op jit(solution)/shard_map/slice | solution.py:96
  321.1 19.7 %collective-permute-start.3 = (f32[2,1,128,128]{3,2,1,0:T(8,128)S(1)}, f32[2,1,128,128]{3,2,1,0:T(8,128)S(1)}, u32[]{:S(2)}, u32[]{:S(2)}) collective-permute-start(f32[2,1,128,128]{3,2,1,0:T(8,128)S(1)} %slice.154), channel_id=1, source_target_pairs={{0,1},{1,2},{2,3},{3,4},{4,5},{5,6},{6,7},{7,8},{8,9},{9,10},{10,1... | collective-permute-start | bytes 393224 | tf_op jit(solution)/shard_map/ppermute | solution.py:19
where the time goes:
time: 343 us; the launch traced here: 342 us
  blocking collectives  133 us (39%)
  waiting for transfers between devices  99.5 us (29%)
  starting transfers between devices  81.9 us (24%)
  local copies, waits for them, and re-layouts  10.3 us (3%)
  other arithmetic  8.42 us (2%)
  matrix products  8.42 us (2%)
    ppermute x4, waiting for transfers between devices, from_behind(): return lax.ppermute(block, axis, route)  80.1 us
    all_to_all x2, blocking collectives, data_term(): lax.all_to_all(back_field, 'slab', split_axis=2, concat_axis=3, tiled=True)  60.1 us
    all_to_all x2, starting transfers between devices, sum_at_owner(): lax.all_to_all(tiles, axis, split_axis=0, concat_axis=0, tiled=True)  44.8 us
    all_gather x2, blocking collectives, on_device(): whole_guess = lax.all_gather(guess, 'coil', axis=2, tiled=True)  36.5 us
    all_to_all x1, blocking collectives, data_term(): lax.all_to_all(pieces, 'slab', split_axis=3, concat_axis=2, tiled=True)  35.9 us
    ppermute x4, starting transfers between devices, from_behind(): return lax.ppermute(block, axis, route)  23.5 us
    all_to_all x1, waiting for transfers between devices, data_term(): lax.all_to_all(pieces, 'slab', split_axis=3, concat_axis=2, tiled=True)  19.4 us
    all_to_all x1, starting transfers between devices, data_term(): lax.all_to_all(pieces, 'slab', split_axis=3, concat_axis=2, tiled=True)  13.6 us
  transfers between devices with their start and end apart: 7, of which 5 were waited for; matrix products, arithmetic and copies ran while one was open for 1% of the time, Pallas kernels for 0%

commit v1 on v0

--- a/solution.py
+++ b/solution.py
@@ -133,7 +133,15 @@
     guess = current
     duals = None
     for turn_index in range(ITERS):
-        whole_guess = lax.all_gather(guess, "coil", axis=2, tiled=True)
+        whole_guess = jnp.concatenate(
+            lax.all_to_all(
+                jnp.stack([guess for _ in range(lax.psum(1, axis_name="coil"))], 0),
+                "coil",
+                split_axis=0,
+                concat_axis=0,
+            ),
+            2,
+        )
         if duals is None:
             duals = (
                 jnp.zeros_like(whole_guess),

time: 343 us -> 375 us (1.093)
  waiting for transfers between devices: 99.5 us -> 148 us
  starting transfers between devices: 81.9 us -> 66.2 us
  blocking collectives: 133 us -> 124 us
  local copies, waits for them, and re-layouts: 10.3 us -> 14.9 us
    all_gather x2 -> x0, blocking collectives: 36.5 us -> none  [on_device(): whole_guess = lax.all_gather(guess, 'coil', axis=2, tiled=True)]
    all_to_all x0 -> x1, blocking collectives: none -> 31.2 us  [on_device(): lax.all_to_all(jnp.stack([guess for _ in range(lax.psum(1, axis_name='coi...]
    all_to_all x0 -> x1, waiting for transfers between devices: none -> 23.6 us  [on_device(): lax.all_to_all(jnp.stack([guess for _ in range(lax.psum(1, axis_name='coi...]
    all_to_all x2, starting transfers between devices: 44.8 us -> 28.1 us  [sum_at_owner(): lax.all_to_all(tiles, axis, split_axis=0, concat_axis=0, tiled=True)]
    all_to_all x1, waiting for transfers between devices: 19.4 us -> 32.2 us  [data_term(): lax.all_to_all(pieces, 'slab', split_axis=3, concat_axis=2, tiled=True)]
    ppermute x4, waiting for transfers between devices: 80.1 us -> 92.5 us  [from_behind(): return lax.ppermute(block, axis, route)]
    all_to_all x0 -> x1, starting transfers between devices: none -> 11.3 us  [on_device(): lax.all_to_all(jnp.stack([guess for _ in range(lax.psum(1, axis_name='coi...]
    ppermute x4, starting transfers between devices: 23.5 us -> 13.3 us  [from_behind(): return lax.ppermute(block, axis, route)]
  transfers between devices with their start and end apart: 7 -> 8, of which waited for: 5 -> 6; matrix products, arithmetic and copies ran while one was open for 1% -> 2% of each run, Pallas kernels for 0% -> 0%
where the time goes in v1:
time: 375 us; the launch traced here: 374 us
  waiting for transfers between devices  148 us (39%)
  blocking collectives  124 us (33%)
  starting transfers between devices  66.2 us (18%)
  local copies, waits for them, and re-layouts  14.9 us (4%)
  other arithmetic  11.4 us (3%)
  matrix products  8.69 us (2%)
    ppermute x4, waiting for transfers between devices, from_behind(): return lax.ppermute(block, axis, route)  92.5 us
    all_to_all x2, blocking collectives, data_term(): lax.all_to_all(back_field, 'slab', split_axis=2, concat_axis=3, tiled=True)  57 us
    all_to_all x1, blocking collectives, data_term(): lax.all_to_all(pieces, 'slab', split_axis=3, concat_axis=2, tiled=True)  35.8 us
    all_to_all x1, waiting for transfers between devices, data_term(): lax.all_to_all(pieces, 'slab', split_axis=3, concat_axis=2, tiled=True)  32.2 us
    all_to_all x1, blocking collectives, on_device(): lax.all_to_all(jnp.stack([guess for _ in range(lax.psum(1, axis_name='coi...  31.2 us
    all_to_all x2, starting transfers between devices, sum_at_owner(): lax.all_to_all(tiles, axis, split_axis=0, concat_axis=0, tiled=True)  28.1 us
    all_to_all x1, waiting for transfers between devices, on_device(): lax.all_to_all(jnp.stack([guess for _ in range(lax.psum(1, axis_name='coi...  23.6 us
    all_to_all x1, starting transfers between devices, data_term(): lax.all_to_all(pieces, 'slab', split_axis=3, concat_axis=2, tiled=True)  13.5 us
  transfers between devices with their start and end apart: 8, of which 6 were waited for; matrix products, arithmetic and copies ran while one was open for 2% of the time, Pallas kernels for 0%

profile of v1, /device:TPU:130, one launch (start us, length us, event | category | flops | bytes accessed | tf_op | source)
XLA Modules:
  0.0 374.1 jit_solution(3714179130609600074)
XLA Ops:
  0.0 1.6 stack.62
  1.6 11.3 %all-to-all-start = ((f32[16,2,4,8,128]{4,3,2,1,0:T(8,128)}), f32[16,2,4,8,128]{4,3,2,1,0:T(8,128)S(1)}, u32[]{:S(2)}, u32[]{:S(2)}) async-start(f32[16,2,4,8,128]{4,3,2,1,0:T(8,128)} %stack.62), calls=%async_computation | async-start | bytes 1048576 | tf_op jit(solution)/shard_map/all_to_all | solution.py:137
  12.9 0.3 fusion.109
  13.2 0.3 negate_convert_fusion
  13.5 23.6 %all-to-all-done = f32[16,2,4,8,128]{4,3,2,1,0:T(8,128)S(1)} async-done(((f32[16,2,4,8,128]{4,3,2,1,0:T(8,128)}), f32[16,2,4,8,128]{4,3,2,1,0:T(8,128)S(1)}, u32[]{:S(2)}, u32[]{:S(2)}) %all-to-all-start) | async-done | bytes 524320 | tf_op jit(solution)/shard_map/all_to_all | solution.py:137
  37.2 1.0 copy-done
  38.2 0.2 fusion.24
  38.4 0.6 fusion.21
  39.0 1.2 copy.82
  40.2 13.5 %all-to-all-start.1 = ((bf16[2,2,4,128,128]{4,2,0,1,3:T(4,128)(2,1)}), bf16[2,2,4,128,128]{4,2,0,1,3:T(4,128)(2,1)S(1)}, u32[]{:S(2)}, u32[]{:S(2)}) async-start(bf16[2,2,4,128,128]{4,2,0,1,3:T(4,128)(2,1)} %copy.82), calls=%async_computation.1 | async-start | bytes 1048576 | tf_op jit(solution)/shard_map/all_to_all | solution.py:62
  53.7 32.2 %all-to-all-done.1 = bf16[2,2,4,128,128]{4,2,0,1,3:T(4,128)(2,1)S(1)} async-done(((bf16[2,2,4,128,128]{4,2,0,1,3:T(4,128)(2,1)}), bf16[2,2,4,128,128]{4,2,0,1,3:T(4,128)(2,1)S(1)}, u32[]{:S(2)}, u32[]{:S(2)}) %all-to-all-start.1) | async-done | bytes 524320 | tf_op jit(solution)/shard_map/all_to_all | solution.py:62
  85.9 0.2 copy.83
  86.2 0.8 copy-done.16
  86.9 1.3 fusion.130
  88.3 0.3 fusion.20
  88.6 0.4 copy.87
  89.0 28.5 %all_to_all.92 = bf16[2,2,128,4,128]{4,3,0,1,2:T(4,128)(2,1)S(1)} all-to-all(bf16[2,2,128,4,128]{4,3,0,1,2:T(4,128)(2,1)S(1)} %copy.87), channel_id=1, replica_groups=mesh['coil'=16,'slab'=32] {'slab'}, dimensions={2} | all-to-all | bytes 1048576 | tf_op jit(solution)/shard_map/all_to_all | solution.py:78
  117.5 0.2 copy.88
  117.8 0.5 convolution_bitcast_fusion.2
  118.3 0.2 fusion.28
  118.5 0.9 copy.97
  119.4 14.0 %all-to-all-start.3 = ((f32[16,2,4,8,128]{4,3,2,1,0:T(8,128)}), f32[16,2,4,8,128]{4,3,2,1,0:T(8,128)S(1)}, u32[]{:S(2)}, u32[]{:S(2)}) async-start(f32[16,2,4,8,128]{4,3,2,1,0:T(8,128)} %copy.97), calls=%async_computation.3 | async-start | bytes 1048576 | tf_op jit(solution)/shard_map/all_to_all | solution.py:29
  133.4 4.7 %collective-permute-start = (f32[2,1,128,128]{3,2,1,0:T(8,128)S(1)}, f32[2,1,128,128]{3,2,1,0:T(8,128)S(1)}, u32[]{:S(2)}, u32[]{:S(2)}) collective-permute-start(f32[2,1,128,128]{3,2,1,0:T(8,128)S(1)} %slice.139), channel_id=1, source_target_pairs={{1,0},{2,1},{3,2},{4,3},{5,4},{6,5},{7,6},{8,7},{9,8},{10,9},{11,1... | collective-permute-start | bytes 393224 | tf_op jit(solution)/shard_map/ppermute | solution.py:19
  138.1 0.2 slice_subtract_fusion.2
  138.4 0.1 multiply_reduce_fusion.2
  138.6 27.6 %collective-permute-done = f32[2,1,128,128]{3,2,1,0:T(8,128)S(1)} collective-permute-done((f32[2,1,128,128]{3,2,1,0:T(8,128)S(1)}, f32[2,1,128,128]{3,2,1,0:T(8,128)S(1)}, u32[]{:S(2)}, u32[]{:S(2)}) %collective-permute-start) | collective-permute-done | bytes 131104 | tf_op jit(solution)/shard_map/ppermute | solution.py:19
  166.2 0.2 multiply_reduce_fusion.4
  166.5 0.1 fusion.88
  166.6 0.5 copy-done.7
  167.1 0.3 fusion.44
  167.5 0.7 slice.144
  168.2 1.9 collective-permute-start.1
  170.1 0.8 slice.145
  170.9 0.6 reduce_sum.118
  171.5 19.5 %collective-permute-done.1 = f32[2,1,128,128]{3,2,1,0:T(8,128)} collective-permute-done((f32[2,1,128,128]{3,2,1,0:T(8,128)}, f32[2,1,128,128]{3,2,1,0:T(8,128)}, u32[]{:S(2)}, u32[]{:S(2)}) %collective-permute-start.1) | collective-permute-done | bytes 131104 | tf_op jit(solution)/shard_map/ppermute | solution.py:19
  191.0 1.5 multiply_subtract_fusion.1
  192.5 31.2 %all_to_all.93 = f32[16,2,4,8,128]{4,3,2,1,0:T(8,128)S(1)} all-to-all(f32[16,2,4,8,128]{4,3,2,1,0:T(8,128)S(1)} %stack.67), channel_id=1, replica_groups=mesh['coil'=16,'slab'=32] {'coil'}, dimensions={0} | all-to-all | bytes 1048576 | tf_op jit(solution)/shard_map/all_to_all | solution.py:137
  223.9 1.0 fusion.32
  224.9 2.6 fusion.18
  227.4 1.4 copy.100
  228.9 35.8 %all_to_all.94 = bf16[2,2,4,128,128]{4,2,0,1,3:T(4,128)(2,1)S(1)} all-to-all(bf16[2,2,4,128,128]{4,2,0,1,3:T(4,128)(2,1)S(1)} %copy.100), channel_id=1, replica_groups=mesh['coil'=16,'slab'=32] {'slab'}, dimensions={3} | all-to-all | bytes 1048576 | tf_op jit(solution)/shard_map/all_to_all | solution.py:62
  264.7 0.2 copy.101
  264.9 0.8 copy-done.17
  265.7 0.4 fusion.6
  266.2 0.4 copy-done.4
  266.6 0.3 fusion.17
  266.9 0.4 copy.105
  267.3 28.5 %all_to_all.95 = bf16[2,2,128,4,128]{4,3,0,1,2:T(4,128)(2,1)S(1)} all-to-all(bf16[2,2,128,4,128]{4,3,0,1,2:T(4,128)(2,1)S(1)} %copy.105), channel_id=1, replica_groups=mesh['coil'=16,'slab'=32] {'slab'}, dimensions={2} | all-to-all | bytes 1048576 | tf_op jit(solution)/shard_map/all_to_all | solution.py:78
  295.8 1.1 copy.106
  296.9 2.7 convolution_bitcast_fusion
  299.6 1.4 fusion.36
  301.0 0.9 copy.115
  301.9 14.1 %all-to-all-start.7 = ((f32[16,2,4,8,128]{4,3,2,1,0:T(8,128)}), f32[16,2,4,8,128]{4,3,2,1,0:T(8,128)}, u32[]{:S(2)}, u32[]{:S(2)}) async-start(f32[16,2,4,8,128]{4,3,2,1,0:T(8,128)} %copy.115), calls=%async_computation.7 | async-start | bytes 1048576 | tf_op jit(solution)/shard_map/all_to_all | solution.py:29
  316.1 1.1 fusion.82
  317.2 4.7 %collective-permute-start.2 = (f32[2,1,128,128]{3,2,1,0:T(8,128)S(1)}, f32[2,1,128,128]{3,2,1,0:T(8,128)S(1)}, u32[]{:S(2)}, u32[]{:S(2)}) collective-permute-start(f32[2,1,128,128]{3,2,1,0:T(8,128)S(1)} %slice.153), channel_id=1, source_target_pairs={{1,0},{2,1},{3,2},{4,3},{5,4},{6,5},{7,6},{8,7},{9,8},{10,9},{11,1... | collective-permute-start | bytes 393224 | tf_op jit(solution)/shard_map/ppermute | solution.py:19
  321.8 0.2 slice_subtract_fusion
  322.4 26.5 %collective-permute-done.2 = f32[2,1,128,128]{3,2,1,0:T(8,128)S(1)} collective-permute-done((f32[2,1,128,128]{3,2,1,0:T(8,128)S(1)}, f32[2,1,128,128]{3,2,1,0:T(8,128)S(1)}, u32[]{:S(2)}, u32[]{:S(2)}) %collective-permute-start.2) | collective-permute-done | bytes 131104 | tf_op jit(solution)/shard_map/ppermute | solution.py:19
  348.9 0.2 fusion.58
  349.3 0.9 copy-done.2
  350.2 1.1 fusion.53
  351.4 2.1 collective-permute-start.3
  353.5 1.1 reduce_sum.125
  354.6 18.8 %collective-permute-done.3 = f32[2,1,128,128]{3,2,1,0:T(8,128)S(1)} collective-permute-done((f32[2,1,128,128]{3,2,1,0:T(8,128)S(1)}, f32[2,1,128,128]{3,2,1,0:T(8,128)S(1)}, u32[]{:S(2)}, u32[]{:S(2)}) %collective-permute-start.3) | collective-permute-done | bytes 131104 | tf_op jit(solution)/shard_map/ppermute | solution.py:19
  373.4 0.7 multiply_subtract_fusion
  (65 shorter events, 1.0 us)
Async XLA Ops:
  1.6 35.5 %all-to-all-start = ((f32[16,2,4,8,128]{4,3,2,1,0:T(8,128)}), f32[16,2,4,8,128]{4,3,2,1,0:T(8,128)S(1)}, u32[]{:S(2)}, u32[]{:S(2)}) async-start(f32[16,2,4,8,128]{4,3,2,1,0:T(8,128)} %stack.62), calls=%async_computation | async-start | bytes 1048576 | tf_op jit(solution)/shard_map/all_to_all | solution.py:137
  13.5 72.7 %copy-start.18 = (bf16[1,2,128,128]{2,3,0,1:T(8,128)(2,1)}, bf16[1,2,128,128]{2,3,0,1:T(8,128)(2,1)S(1)}, u32[]{:S(2)}) copy-start(bf16[1,2,128,128]{2,3,0,1:T(8,128)(2,1)S(1)} %get-tuple-element.34) | copy-start | bytes 196612
  13.5 72.7 %copy-start.20 = (bf16[1,2,128,128]{2,3,0,1:T(8,128)(2,1)}, bf16[1,2,128,128]{2,3,0,1:T(8,128)(2,1)S(1)}, u32[]{:S(2)}) copy-start(bf16[1,2,128,128]{2,3,0,1:T(8,128)(2,1)S(1)} %get-tuple-element.37) | copy-start | bytes 196612
  13.5 104.3 %copy-start.3 = (bf16[1,2,128,128]{2,3,1,0:T(8,128)(2,1)}, bf16[1,2,128,128]{2,3,1,0:T(8,128)(2,1)S(1)}, u32[]{:S(2)}) copy-start(bf16[1,2,128,128]{2,3,1,0:T(8,128)(2,1)S(1)} %get-tuple-element.33) | copy-start | bytes 196612
  13.5 104.3 %copy-start.5 = (bf16[1,2,128,128]{2,3,1,0:T(8,128)(2,1)}, bf16[1,2,128,128]{2,3,1,0:T(8,128)(2,1)S(1)}, u32[]{:S(2)}) copy-start(bf16[1,2,128,128]{2,3,1,0:T(8,128)(2,1)S(1)} %get-tuple-element.38) | copy-start | bytes 196612
  37.2 1.0 copy-start
  40.2 13.5 %copy-start.23 = (s32[2,128,4]{1,2,0:T(4,128)S(1)}, s32[2,128,4]{1,2,0:T(4,128)}, u32[]{:S(2)}) copy-start(s32[2,128,4]{1,2,0:T(4,128)} %param.6) | copy-start | bytes 12292
  40.2 45.7 %all-to-all-start.1 = ((bf16[2,2,4,128,128]{4,2,0,1,3:T(4,128)(2,1)}), bf16[2,2,4,128,128]{4,2,0,1,3:T(4,128)(2,1)S(1)}, u32[]{:S(2)}, u32[]{:S(2)}) async-start(bf16[2,2,4,128,128]{4,2,0,1,3:T(4,128)(2,1)} %copy.82), calls=%async_computation.1 | async-start | bytes 1048576 | tf_op jit(solution)/shard_map/all_to_all | solution.py:62
  85.9 1.0 copy-start.16
  119.4 51.5 %all-to-all-start.3 = ((f32[16,2,4,8,128]{4,3,2,1,0:T(8,128)}), f32[16,2,4,8,128]{4,3,2,1,0:T(8,128)S(1)}, u32[]{:S(2)}, u32[]{:S(2)}) async-start(f32[16,2,4,8,128]{4,3,2,1,0:T(8,128)} %copy.97), calls=%async_computation.3 | async-start | bytes 1048576 | tf_op jit(solution)/shard_map/all_to_all | solution.py:29
  133.4 32.8 %collective-permute-start = (f32[2,1,128,128]{3,2,1,0:T(8,128)S(1)}, f32[2,1,128,128]{3,2,1,0:T(8,128)S(1)}, u32[]{:S(2)}, u32[]{:S(2)}) collective-permute-start(f32[2,1,128,128]{3,2,1,0:T(8,128)S(1)} %slice.139), channel_id=1, source_target_pairs={{1,0},{2,1},{3,2},{4,3},{5,4},{6,5},{7,6},{8,7},{9,8},{10,9},{11,1... | collective-permute-start | bytes 393224 | tf_op jit(solution)/shard_map/ppermute | solution.py:19
  138.6 27.9 %copy-start.9 = (f32[4,128,128]{2,1,0:T(8,128)}, f32[4,128,128]{2,1,0:T(8,128)S(1)}, u32[]{:S(2)}) copy-start(f32[4,128,128]{2,1,0:T(8,128)S(1)} %get-tuple-element.43) | copy-start | bytes 786436
  138.6 27.9 %copy-start.11 = (f32[4,128,128]{2,1,0:T(8,128)}, f32[4,128,128]{2,1,0:T(8,128)S(1)}, u32[]{:S(2)}) copy-start(f32[4,128,128]{2,1,0:T(8,128)S(1)} %get-tuple-element.44) | copy-start | bytes 786436
  166.2 0.9 copy-start.13
  166.4 0.7 copy-start.7
  167.4 23.6 %copy-start.1 = (f32[2,4,128,128]{3,2,1,0:T(8,128)}, f32[2,4,128,128]{3,2,1,0:T(8,128)S(1)}, u32[]{:S(2)}) copy-start(f32[2,4,128,128]{3,2,1,0:T(8,128)S(1)} %get-tuple-element.30) | copy-start | bytes 1572868
  168.2 22.8 %collective-permute-start.1 = (f32[2,1,128,128]{3,2,1,0:T(8,128)}, f32[2,1,128,128]{3,2,1,0:T(8,128)}, u32[]{:S(2)}, u32[]{:S(2)}) collective-permute-start(f32[2,1,128,128]{3,2,1,0:T(8,128)} %slice.144), channel_id=1, source_target_pairs={{0,1},{1,2},{2,3},{3,4},{4,5},{5,6},{6,7},{7,8},{8,9},{9,10},{10,1... | collective-permute-start | bytes 393224 | tf_op jit(solution)/shard_map/ppermute | solution.py:19
  228.9 36.0 %copy-start.15 = (f32[2,2,128,4,128]{4,2,3,0,1:T(8,128)S(1)}, f32[2,2,128,4,128]{4,2,3,0,1:T(8,128)}, u32[]{:S(2)}) copy-start(f32[2,2,128,4,128]{4,2,3,0,1:T(8,128)} %get-tuple-element.40) | copy-start | bytes 3145732
  264.7 1.0 copy-start.17
  264.7 1.0 copy-start.19
  264.7 1.0 copy-start.21
  265.7 0.8 copy-start.4
  265.7 0.9 copy-start.6
  301.9 14.1 %copy-start.8 = (f32[4,16,8,128]{3,2,1,0:T(8,128)S(1)}, f32[4,16,8,128]{3,2,1,0:T(8,128)}, u32[]{:S(2)}) copy-start(f32[4,16,8,128]{3,2,1,0:T(8,128)} %copy-done.7) | copy-start | bytes 786436
  301.9 14.1 %copy-start.10 = (f32[4,128,128]{2,1,0:T(8,128)S(1)}, f32[4,128,128]{2,1,0:T(8,128)}, u32[]{:S(2)}) copy-start(f32[4,128,128]{2,1,0:T(8,128)} %copy-done.9) | copy-start | bytes 786436
  301.9 51.6 %all-to-all-start.7 = ((f32[16,2,4,8,128]{4,3,2,1,0:T(8,128)}), f32[16,2,4,8,128]{4,3,2,1,0:T(8,128)}, u32[]{:S(2)}, u32[]{:S(2)}) async-start(f32[16,2,4,8,128]{4,3,2,1,0:T(8,128)} %copy.115), calls=%async_computation.7 | async-start | bytes 1048576 | tf_op jit(solution)/shard_map/all_to_all | solution.py:29
  317.2 31.7 %collective-permute-start.2 = (f32[2,1,128,128]{3,2,1,0:T(8,128)S(1)}, f32[2,1,128,128]{3,2,1,0:T(8,128)S(1)}, u32[]{:S(2)}, u32[]{:S(2)}) collective-permute-start(f32[2,1,128,128]{3,2,1,0:T(8,128)S(1)} %slice.153), channel_id=1, source_target_pairs={{1,0},{2,1},{3,2},{4,3},{5,4},{6,5},{7,6},{8,7},{9,8},{10,9},{11,1... | collective-permute-start | bytes 393224 | tf_op jit(solution)/shard_map/ppermute | solution.py:19
  322.3 26.6 %copy-start.14 = (f32[2,1,128,128]{3,2,1,0:T(8,128)S(1)}, f32[2,1,128,128]{3,2,1,0:T(8,128)}, u32[]{:S(2)}) copy-start(f32[2,1,128,128]{3,2,1,0:T(8,128)} %copy-done.13) | copy-start | bytes 393220
  349.1 1.0 copy-start.2
  351.3 22.1 %copy-start.12 = (f32[2,4,128,128]{3,2,1,0:T(8,128)S(1)}, f32[2,4,128,128]{3,2,1,0:T(8,128)}, u32[]{:S(2)}) copy-start(f32[2,4,128,128]{3,2,1,0:T(8,128)} %get-tuple-element.29) | copy-start | bytes 1572868
  351.4 22.0 %collective-permute-start.3 = (f32[2,1,128,128]{3,2,1,0:T(8,128)S(1)}, f32[2,1,128,128]{3,2,1,0:T(8,128)S(1)}, u32[]{:S(2)}, u32[]{:S(2)}) collective-permute-start(f32[2,1,128,128]{3,2,1,0:T(8,128)S(1)} %slice.158), channel_id=1, source_target_pairs={{0,1},{1,2},{2,3},{3,4},{4,5},{5,6},{6,7},{7,8},{8,9},{9,10},{10,1... | collective-permute-start | bytes 393224 | tf_op jit(solution)/shard_map/ppermute | solution.py:19
  353.4 20.0 %copy-start.22 = (f32[2,4,8,128]{3,2,1,0:T(8,128)S(1)}, f32[2,4,8,128]{3,2,1,0:T(8,128)}, u32[]{:S(2)}) copy-start(f32[2,4,8,128]{3,2,1,0:T(8,128)} %get-tuple-element.10) | copy-start | bytes 98308
